TPU v7x, 1024 devices: a whole 4x4x32 slice. The times are simulated.
1024 devices in a mesh: domain: 32 (over x, y, core), member: 32 (over z).
Axes of the slice: x: 4, y: 4, z: 32, core: 2. Of those that a mesh axis runs over, the one named last changes fastest.
Arguments:
- state: bfloat16 [256, 2048, 256], P('member', 'domain'), may hold values from -6 to 6
- obs_ens: bfloat16 [256, 65536], P('member', 'domain'), may hold values from -6 to 6
- y_obs: bfloat16 [65536], P('domain'), may hold values from -12 to 12
- obs_rinv: bfloat16 [65536], P('domain'), may hold values from 0.29882812 to 3
- block_list: int32 [2048, 8], P('domain'), may hold values from 0 to 1023, as said below
- loc_class: int32 [2048, 8], P('domain'), may hold values from 0 to 7
- loc_table: float32 [8], replicated, may hold values from 0.1 to 1
- patch_active: int32 [2048], P('domain'), may hold values from 0 to 1, as said below
Outputs:
- analysis: bfloat16 [256, 2048, 256], P('member', 'domain')
Inputs may be any that keep to these rules, and one draw needn't show every extreme that they name: `block_list`: the 8 blocks of a patch are distinct, and for a patch of domain group g (patches g * 64 to (g + 1) * 64 - 1) they lie among blocks g * 32 - 6 to (g + 1) * 32 + 5. `patch_active`: exactly 32 of the 64 patches of each domain group are 1.
All inputs are finite; a program needn't handle non-finite values.
Results may differ from a plain program's by a relative error of at most 0.015.
Values may be sent and summed in bfloat16 or wider, within the bound.
A program may use at most 32 MiB of HBM per device.

v0:
```python
import jax
import jax.numpy as jnp
from jax import lax
from jax.sharding import PartitionSpec as P

BROWS = 64
HB = 6
BLK_DOM = 32
APD = 1
NEWTON = 6
OBS_ROWS = 512


def padded(array, sides, width):
    for axis, dim in sides:
        devices, length = (lax.axis_size(axis), array.shape[dim])
        up = [(i, (i + 1) % devices) for i in range(devices - 1)]
        down = [(j, i) for i, j in up]
        last = lax.slice_in_dim(array, length - width, length, axis=dim)
        leading = lax.slice_in_dim(array, 0, width, axis=dim)
        before = lax.ppermute(last, axis, up)
        after = lax.ppermute(leading, axis, down)
        array = jnp.concatenate([before, array, after], axis=dim)
    return array


def make_transform(obs_sel, y_sel, rinv_sel, loc_rows):
    count = obs_sel.shape[0]
    ones_row = jnp.ones((count,), jnp.bfloat16)
    obs_mean = jnp.dot(ones_row, obs_sel, preferred_element_type=jnp.float32) / count
    obs_pert = (obs_sel - obs_mean).astype(jnp.bfloat16)
    row_weight = rinv_sel.astype(jnp.float32) * loc_rows
    weighted = (obs_pert * row_weight).astype(jnp.bfloat16)
    gram = lax.dot_general(
        weighted, obs_pert, (((1,), (1,)), ((), ())), preferred_element_type=jnp.float32
    )
    identity = jnp.eye(count, dtype=jnp.float32)
    system = identity + gram / (count - 1)
    innovation = y_sel.astype(jnp.float32) - obs_mean
    projected = jnp.dot(weighted.astype(jnp.float32), innovation, precision=lax.Precision.HIGHEST)
    frobenius = jnp.sqrt(jnp.sum(system * system))
    iter_y = system / frobenius
    iter_z = identity
    for step in range(NEWTON):
        halfway = 1.5 * identity - 0.5 * jnp.dot(iter_z, iter_y, precision=lax.Precision.HIGHEST)
        iter_y = jnp.dot(iter_y, halfway, precision=lax.Precision.HIGHEST)
        iter_z = jnp.dot(halfway, iter_z, precision=lax.Precision.HIGHEST)
    inner = jnp.dot(iter_z, projected, precision=lax.Precision.HIGHEST)
    mean_weight = jnp.dot(iter_z, inner, precision=lax.Precision.HIGHEST) / (
        frobenius * (count - 1)
    )
    return (iter_z / jnp.sqrt(frobenius) + mean_weight[:, None]).astype(jnp.bfloat16)


def apply_transform(transform, members_state):
    count = members_state.shape[0]
    ones_row = jnp.ones((count,), jnp.bfloat16)
    state_mean = jnp.dot(ones_row, members_state, preferred_element_type=jnp.float32) / count
    state_pert = (members_state - state_mean).astype(jnp.bfloat16)
    update = lax.dot_general(
        transform, state_pert, (((0,), (0,)), ((), ())), preferred_element_type=jnp.float32
    )
    return (state_mean + update).astype(jnp.bfloat16)


def per_device(state, obs_ens, y_obs, obs_rinv, block_list, loc_class, loc_table, patch_active):
    mem_local = state.shape[0]
    width = state.shape[2]
    members = lax.axis_size("member")
    owner = lax.axis_index("member")
    group = lax.axis_index("domain")
    stacked = jnp.concatenate([obs_ens, y_obs[None, :], obs_rinv[None, :]], axis=0)
    extended = padded(stacked, (("domain", 1),), HB * BROWS)
    blocks = extended.reshape(mem_local + 2, -1, BROWS)
    local_ids = block_list - (group * BLK_DOM - HB)
    classes = jnp.arange(loc_table.shape[0], dtype=jnp.int32)
    loc_weight = jnp.sum(
        jnp.where(loc_class[..., None] == classes, loc_table, jnp.float32(0.0)), axis=-1
    )
    selected = jnp.argsort(1 - patch_active, stable=True)[: APD * members]
    routed_state = jnp.take(state, selected, axis=1)
    per_owner = selected.shape[0] // members
    picked = jnp.take(blocks, local_ids[selected], axis=1)
    rows = OBS_ROWS
    obs_send = picked[:mem_local].reshape(mem_local, members, per_owner, rows)
    state_send = routed_state.reshape(mem_local, members, per_owner, width)
    obs_here, state_here = (
        lax.all_to_all(obs_send, "member", split_axis=1, concat_axis=0, tiled=True),
        lax.all_to_all(state_send, "member", split_axis=1, concat_axis=0, tiled=True),
    )
    y_mine = lax.dynamic_slice_in_dim(
        picked[mem_local].reshape(-1, rows), owner * per_owner, per_owner, 0
    )
    rinv_mine = lax.dynamic_slice_in_dim(
        picked[mem_local + 1].reshape(-1, rows), owner * per_owner, per_owner, 0
    )
    weight_mine = lax.dynamic_slice_in_dim(loc_weight[selected], owner * per_owner, per_owner, 0)
    loc_rows = jnp.broadcast_to(
        weight_mine[:, :, None], (per_owner, weight_mine.shape[1], BROWS)
    ).reshape(per_owner, rows)
    transforms = jax.vmap(make_transform, in_axes=(1, 0, 0, 0), out_axes=0)(
        obs_here[:, 0], y_mine, rinv_mine, loc_rows
    )
    analysed = jax.vmap(apply_transform, in_axes=(0, 1), out_axes=1)(transforms, state_here[:, 0])
    returned = lax.all_to_all(analysed[:, None], "member", split_axis=0, concat_axis=1, tiled=True)
    returned = returned.reshape(mem_local, members * per_owner, width)
    return state.at[:, selected].set(returned)


def solution(mesh):
    placed = (
        P("member", "domain", None),
        P("member", "domain"),
        P("domain"),
        P("domain"),
        P("domain", None),
        P("domain", None),
        P(),
        P("domain"),
    )
    return jax.shard_map(
        per_device,
        mesh=mesh,
        in_specs=placed,
        out_specs=P("member", "domain", None),
        check_vma=False,
    )
```

profile of v0, /device:TPU:1, one launch (start us, length us, event | category | flops | bytes accessed | tf_op | source)
XLA Modules:
  0.0 168.7 jit_solution(6389250572455177669)
XLA Ops:
  0.0 1.0 copy.73
  1.0 0.7 copy-done.3
  1.7 4.6 %collective-permute-start = (bf16[10,384]{1,0:T(8,128)(2,1)S(1)}, bf16[10,384]{1,0:T(8,128)(2,1)S(1)}, u32[]{:S(2)}, u32[]{:S(2)}) collective-permute-start(bf16[10,384]{1,0:T(8,128)(2,1)S(1)} %get-tuple-element.11), channel_id=1, source_target_pairs={{0,32},{32,64},{64,96},{96,128},{128,160},{160,192},{192,224},{224... | collective-permute-start | bytes 23048 | tf_op jit(solution)/shard_map/ppermute | solution.py:21
  6.3 12.8 %collective-permute-start.1 = (bf16[10,384]{1,0:T(8,128)(2,1)S(1)}, bf16[10,384]{1,0:T(8,128)(2,1)S(1)}, u32[]{:S(2)}, u32[]{:S(2)}) collective-permute-start(bf16[10,384]{1,0:T(8,128)(2,1)S(1)} %get-tuple-element.12), channel_id=1, source_target_pairs={{32,0},{64,32},{96,64},{128,96},{160,128},{192,160},{224,192},{256... | collective-permute-start | bytes 23048 | tf_op jit(solution)/shard_map/ppermute | solution.py:22
  19.1 2.1 %sort.17 = (s32[64]{0:T(128)}, s32[64]{0:T(128)S(1)}) sort(s32[64]{0:T(128)S(1)} %broadcast_subtract_fusion.1, s32[64]{0:T(128)S(1)} %iota.54), dimensions={0}, to_apply=%region_0.1 | sort | flops 384 | bytes 1024 | tf_op jit(solution)/shard_map/jit(argsort)/sort | solution.py:80
  21.2 0.9 gather_fusion
  22.3 0.7 copy.55
  23.0 17.6 %all-to-all-start = ((bf16[8,32,1,256]{3,0,2,1:T(8,128)(2,1)}), bf16[8,32,1,256]{3,0,2,1:T(8,128)(2,1)S(1)}, u32[]{:S(2)}, u32[]{:S(2)}) async-start(bf16[8,32,1,256]{3,0,2,1:T(8,128)(2,1)} %copy.55), calls=%async_computation | async-start | bytes 262144 | tf_op jit(solution)/shard_map/all_to_all | solution.py:89
  40.7 0.7 copy-done.4
  41.4 0.6 gather_fusion.1
  42.4 0.8 gather_fusion.2
  43.8 0.8 copy.63
  44.6 26.4 %all-to-all-done = bf16[8,32,1,256]{3,0,2,1:T(8,128)(2,1)S(1)} async-done(((bf16[8,32,1,256]{3,0,2,1:T(8,128)(2,1)}), bf16[8,32,1,256]{3,0,2,1:T(8,128)(2,1)S(1)}, u32[]{:S(2)}, u32[]{:S(2)}) %all-to-all-start) | async-done | bytes 131104 | tf_op jit(solution)/shard_map/all_to_all | solution.py:89
  71.0 3.9 %all-to-all-start.1 = ((bf16[8,32,1,512]{3,0,2,1:T(8,128)(2,1)}), bf16[8,32,1,512]{3,0,2,1:T(8,128)(2,1)S(1)}, u32[]{:S(2)}, u32[]{:S(2)}) async-start(bf16[8,32,1,512]{3,0,2,1:T(8,128)(2,1)} %copy.63), calls=%async_computation.1 | async-start | bytes 524288 | tf_op jit(solution)/shard_map/all_to_all | solution.py:88
  74.9 0.7 copy-done.5
  75.8 0.6 gather_fusion.3
  76.9 40.1 %all-to-all-done.1 = bf16[8,32,1,512]{3,0,2,1:T(8,128)(2,1)S(1)} async-done(((bf16[8,32,1,512]{3,0,2,1:T(8,128)(2,1)}), bf16[8,32,1,512]{3,0,2,1:T(8,128)(2,1)S(1)}, u32[]{:S(2)}, u32[]{:S(2)}) %all-to-all-start.1) | async-done | bytes 262176 | tf_op jit(solution)/shard_map/all_to_all | solution.py:88
  117.2 1.0 multiply_reduce_fusion
  119.3 0.4 fusion.23
  119.9 0.4 fusion.4
  121.1 0.4 fusion.3
  121.5 0.4 fusion.38
  122.3 0.4 fusion.2
  122.6 0.4 fusion.40
  123.0 0.4 fusion.39
  123.4 0.4 fusion.1
  124.2 0.4 fusion.41
  124.6 0.4 fusion
  126.7 0.6 broadcast.197
  127.3 0.7 reduce.2
  128.1 34.0 %all_to_all.45 = bf16[32,2,1024]{2,1,0:T(2,128)(2,1)S(1)} all-to-all(bf16[32,2,1024]{2,1,0:T(2,128)(2,1)S(1)} %reshape.389), channel_id=1, replica_groups=mesh['domain'=32,'member'=32] {'member'}, dimensions={0} | all-to-all | bytes 262144 | tf_op jit(solution)/shard_map/all_to_all | solution.py:105
  162.2 6.5 %scatter_fusion = bf16[8,64,256]{2,1,0:T(8,128)(2,1)} fusion(bf16[8,64,256]{2,1,0:T(8,128)(2,1)} %copy-done, s32[32]{0:T(128)S(1)} %get-tuple-element.8, bf16[32,8,256]{2,0,1:T(8,128)(2,1)S(1)} %copy.62), kind=kCustom, calls=%fused_computation.4 | custom fusion | bytes 393344 | tf_op jit(solution)/shard_map/scatter | solution.py:107
  (64 shorter events, 5.9 us)
Async XLA Ops:
  0.0 1.0 copy-start.2
  0.0 1.7 copy-start.1
  1.0 21.2 %copy-start = (bf16[8,64,256]{2,1,0:T(8,128)(2,1)}, bf16[8,64,256]{2,1,0:T(8,128)(2,1)S(1)}, u32[]{:S(2)}) copy-start(bf16[8,64,256]{2,1,0:T(8,128)(2,1)S(1)} %copy.73) | copy-start | bytes 786436
  1.0 0.7 copy-start.3
  1.7 17.4 %copy-start.7 = (s32[64]{0:T(128)S(1)}, s32[64]{0:T(128)}, u32[]{:S(2)}) copy-start(s32[64]{0:T(128)} %param.15) | copy-start | bytes 772
  1.7 40.4 %collective-permute-start = (bf16[10,384]{1,0:T(8,128)(2,1)S(1)}, bf16[10,384]{1,0:T(8,128)(2,1)S(1)}, u32[]{:S(2)}, u32[]{:S(2)}) collective-permute-start(bf16[10,384]{1,0:T(8,128)(2,1)S(1)} %get-tuple-element.11), channel_id=1, source_target_pairs={{0,32},{32,64},{64,96},{96,128},{128,160},{160,192},{192,224},{224... | collective-permute-start | bytes 23048 | tf_op jit(solution)/shard_map/ppermute | solution.py:21
  6.3 35.8 %collective-permute-start.1 = (bf16[10,384]{1,0:T(8,128)(2,1)S(1)}, bf16[10,384]{1,0:T(8,128)(2,1)S(1)}, u32[]{:S(2)}, u32[]{:S(2)}) collective-permute-start(bf16[10,384]{1,0:T(8,128)(2,1)S(1)} %get-tuple-element.12), channel_id=1, source_target_pairs={{32,0},{64,32},{96,64},{128,96},{160,128},{192,160},{224,192},{256... | collective-permute-start | bytes 23048 | tf_op jit(solution)/shard_map/ppermute | solution.py:22
  23.0 48.0 %all-to-all-start = ((bf16[8,32,1,256]{3,0,2,1:T(8,128)(2,1)}), bf16[8,32,1,256]{3,0,2,1:T(8,128)(2,1)S(1)}, u32[]{:S(2)}, u32[]{:S(2)}) async-start(bf16[8,32,1,256]{3,0,2,1:T(8,128)(2,1)} %copy.55), calls=%async_computation | async-start | bytes 262144 | tf_op jit(solution)/shard_map/all_to_all | solution.py:89
  40.7 0.7 copy-start.4
  71.0 46.0 %all-to-all-start.1 = ((bf16[8,32,1,512]{3,0,2,1:T(8,128)(2,1)}), bf16[8,32,1,512]{3,0,2,1:T(8,128)(2,1)S(1)}, u32[]{:S(2)}, u32[]{:S(2)}) async-start(bf16[8,32,1,512]{3,0,2,1:T(8,128)(2,1)} %copy.63), calls=%async_computation.1 | async-start | bytes 524288 | tf_op jit(solution)/shard_map/all_to_all | solution.py:88
  74.9 0.7 copy-start.5
  74.9 0.7 copy-start.6
where the time goes:
time: 169 us
  waiting for transfers between devices  66.6 us (39%)
  starting transfers between devices  38.8 us (23%)
  blocking collectives  34 us (20%)
  local copies, waits for them, and re-layouts  16 us (9%)
  matrix products  8.84 us (5%)
  other arithmetic  3.28 us (2%)
    all_to_all x1, waiting for transfers between devices, per_device(): lax.all_to_all(obs_send, 'member', split_axis=1, concat_axis=0, tiled=True)  40.1 us
    all_to_all x1, blocking collectives, per_device(): lax.all_to_all(analysed[:, None], 'member', split_axis=0, concat_axis=1,...  34 us
    all_to_all x1, waiting for transfers between devices, per_device(): lax.all_to_all(state_send, 'member', split_axis=1, concat_axis=0, tiled=T...  26.4 us
    all_to_all x1, starting transfers between devices, per_device(): lax.all_to_all(state_send, 'member', split_axis=1, concat_axis=0, tiled=T...  17.6 us
    ppermute x1, starting transfers between devices, padded(): after = lax.ppermute(leading, axis, down)  12.8 us
    scatter x1, local copies, waits for them, and re-layouts, per_device(): return state.at[:, selected].set(returned)  6.48 us
    ppermute x1, starting transfers between devices, padded(): before = lax.ppermute(last, axis, up)  4.59 us
    all_to_all x1, starting transfers between devices, per_device(): lax.all_to_all(obs_send, 'member', split_axis=1, concat_axis=0, tiled=True)  3.87 us
  transfers between devices with their start and end apart: 4, of which 2 were waited for; matrix products, arithmetic and copies ran while one was open for 5% of the time, Pallas kernels for 0%

commit v1 on v0

v1 whole, which is shorter than its diff:
```python
import jax
import jax.numpy as jnp
from jax import lax
from jax.experimental import pallas as pl
from jax.experimental.pallas import tpu as pltpu
from jax.sharding import PartitionSpec as P

MESH = pl.DeviceIdType.MESH
F32 = jnp.float32
BF16 = jnp.bfloat16
N = 32
MEM = 8
NS = 256
BROWS = 64
BPP = 8
HB = 6
BLK_DOM = 32
PAT = 64
ROWS = BPP * BROWS
HALO = HB * BROWS
WIDTH = BLK_DOM * BROWS
TILES = (WIDTH + 2 * HALO) // 128
COUNT = N * MEM
NEWTON = 6
STACK = 16
FAR_FIRST = [16] + [s for k in range(15, 0, -1) for s in (k, N - k)]
EARLY = 11


def iota(shape, dim):
    return lax.broadcasted_iota(jnp.int32, shape, dim)


def dot(a, b):
    return jnp.dot(a, b, preferred_element_type=F32)


def split(a):
    high = a.astype(BF16)
    return high, (a - high.astype(F32)).astype(BF16)


def dot3(a, b):
    return dot(a[0], b[0]) + (dot(a[0], b[1]) + dot(a[1], b[0]))


def flat(ref):
    value = ref[...].astype(F32)
    return value.reshape(value.shape[0] * value.shape[1], value.shape[2])


def slabs(value):
    return value.reshape(N, MEM, value.shape[-1]).astype(BF16)


def analyse(obs, yr, loc_rows, y_it, z_it):
    mean = jnp.sum(obs, axis=0, keepdims=True) / COUNT
    pert = (obs - mean).astype(BF16)
    weight = yr[1:2] * loc_rows
    weighted = (pert.astype(F32) * weight).astype(BF16)
    gram = lax.dot_general(weighted, pert, (((1,), (1,)), ((), ())), preferred_element_type=F32)
    eye = (iota((COUNT, COUNT), 0) == iota((COUNT, COUNT), 1)).astype(F32)
    system = eye + gram / (COUNT - 1)
    projected = jnp.sum(weighted.astype(F32) * (yr[0:1] - mean), axis=1, keepdims=True)
    squares = jnp.sum(jnp.sum(system * system, axis=0, keepdims=True), axis=1, keepdims=True)
    fro = jnp.sqrt(squares)
    first = system / fro
    half = 1.5 * eye - 0.5 * first
    y_it[...] = dot3(split(first), split(half))
    z_it[...] = half

    def step(_, carry):
        y, z = split(y_it[...]), split(z_it[...])
        middle = split(1.5 * eye - 0.5 * dot3(z, y))
        y_it[...] = dot3(y, middle)
        z_it[...] = dot3(middle, z)
        return carry

    lax.fori_loop(0, NEWTON - 2, step, 0)
    y, z = split(y_it[...]), split(z_it[...])
    last = dot3(split(1.5 * eye - 0.5 * dot3(z, y)), z)
    z = split(last)
    inner = dot3(z, split(jnp.broadcast_to(projected, (COUNT, COUNT))))
    shift = dot3(z, split(inner)) / (fro * (COUNT - 1))
    return (last / jnp.sqrt(fro) + shift).astype(BF16)


def kernel(
    state_ref, stack_ref, list_ref, class_ref, active_ref, table_ref, out_ref,
    ext, send_o, recv_o, send_s, recv_s, send_r, recv_r, choose, y_it, z_it,
    so_sem, ro_sem, ss_sem, rs_sem, sr_sem, rr_sem, hs_sem, hr_sem,
):
    group, me = lax.axis_index("domain"), lax.axis_index("member")
    right, left = lax.rem(group + 1, N), lax.rem(group + N - 1, N)

    barrier = pltpu.get_barrier_semaphore()
    for k in FAR_FIRST:
        pl.semaphore_signal(
            barrier, inc=1, device_id={"member": lax.rem(me + k, N)}, device_id_type=MESH
        )
    for side in (left, right):
        pl.semaphore_signal(barrier, inc=1, device_id={"domain": side}, device_id_type=MESH)

    def push(src, dst, send_sem, recv_sem, order):
        for k in order:
            peer = lax.rem(me + k, N)
            pltpu.make_async_remote_copy(
                src_ref=src.at[peer], dst_ref=dst.at[me], send_sem=send_sem, recv_sem=recv_sem,
                device_id={"member": peer}, device_id_type=MESH,
            ).start()

    def own(src, dst, recv_sem):
        pltpu.make_async_copy(src.at[me], dst.at[me], recv_sem).start()

    def arrived(dst, recv_sem):
        pltpu.make_async_copy(dst, dst, recv_sem).wait()

    def sent(src, send_sem):
        part = src.at[pl.ds(0, N - 1)]
        pltpu.make_async_copy(part, part, send_sem).wait()

    act = active_ref[...].astype(F32)
    act8 = jnp.broadcast_to(act, (8, PAT))
    wide = (PAT, MEM * PAT)
    upto = (iota(wide, 0) <= iota(wide, 1) % PAT).astype(F32)
    same = (iota(wide, 0) == iota(wide, 1) % PAT).astype(F32)
    rank = dot(act8, upto)[0:1] - 1.0
    live = dot(act8, same)[0:1]
    rank = jnp.where(live > 0.5, rank, -1.0).astype(jnp.int32)
    big = (COUNT, MEM * PAT)
    pick = (rank == iota(big, 0) // MEM) & (iota(big, 1) // PAT == iota(big, 0) % MEM)
    choose[...] = pick.astype(F32).astype(BF16)
    send_s[...] = slabs(dot(choose[...], state_ref[...]))
    ext[:, HALO:HALO + WIDTH] = stack_ref[...]

    ids = (list_ref[...] - (group * BLK_DOM - HB)).astype(F32).astype(BF16)
    rank64 = rank[:, :PAT]
    rows64 = (rank64 == iota((COUNT, PAT), 0) // MEM).astype(F32).astype(BF16)
    listed = dot(rows64, ids).astype(jnp.int32)
    mine = (rank64 == jnp.broadcast_to(me, (8, PAT))).astype(F32).astype(BF16)
    listed_mine = dot(mine, ids).astype(jnp.int32)
    classes = dot(mine, class_ref[...].astype(F32).astype(BF16)).astype(jnp.int32)
    weights = jnp.zeros(classes.shape, F32)
    for c in range(8):
        weights = jnp.where(classes == c, table_ref[c], weights)
    lane = iota((1, ROWS), 1) // BROWS
    loc_rows = jnp.zeros((1, ROWS), F32)
    for b in range(BPP):
        loc_rows = jnp.where(lane == b, weights[0:1, b:b + 1], loc_rows)

    pl.semaphore_wait(barrier, N + 1)

    to_right = pltpu.make_async_remote_copy(
        src_ref=stack_ref.at[:, pl.ds(WIDTH - HALO, HALO)], dst_ref=ext.at[:, pl.ds(0, HALO)],
        send_sem=hs_sem.at[0], recv_sem=hr_sem.at[0],
        device_id={"domain": right}, device_id_type=MESH,
    )
    to_left = pltpu.make_async_remote_copy(
        src_ref=stack_ref.at[:, pl.ds(0, HALO)], dst_ref=ext.at[:, pl.ds(HALO + WIDTH, HALO)],
        send_sem=hs_sem.at[1], recv_sem=hr_sem.at[1],
        device_id={"domain": left}, device_id_type=MESH,
    )
    to_right.start()
    to_left.start()
    own(send_s, recv_s, rs_sem)
    push(send_s, recv_s, ss_sem, rs_sem, FAR_FIRST[:EARLY])
    to_right.wait_recv()
    to_left.wait_recv()

    straight = jnp.concatenate([ext[:, t * 128:(t + 1) * 128] for t in range(TILES)], axis=0)
    turn = (iota((128, 128), 0) == (iota((128, 128), 1) + BROWS) % 128).astype(F32).astype(BF16)
    turned = dot(straight, turn).astype(BF16)
    table = jnp.concatenate([straight, turned], axis=0)
    half_tile = iota((1, 128), 1) < BROWS

    def gather(ids_of, row_in_stack):
        shape = (ids_of.shape[0], 2 * TILES * STACK)
        tiles = []
        for pair in range(BPP // 2):
            sides = []
            for b in (2 * pair, 2 * pair + 1):
                block = ids_of[:, b:b + 1]
                key = (((block + b) & 1) * TILES + (block >> 1)) * STACK + row_in_stack
                hot = (iota(shape, 1) == key).astype(F32).astype(BF16)
                sides.append(dot(hot, table))
            tiles.append(jnp.where(half_tile, sides[0], sides[1]))
        return tiles

    for pair, tile in enumerate(gather(listed, iota((COUNT, 1), 0) % MEM)):
        send_o[:, :, pair * 128:(pair + 1) * 128] = slabs(tile)
    own(send_o, recv_o, ro_sem)
    push(send_o, recv_o, so_sem, ro_sem, FAR_FIRST)
    push(send_s, recv_s, ss_sem, rs_sem, FAR_FIRST[EARLY:])
    yr = jnp.concatenate(gather(listed_mine, MEM + iota((8, 1), 0)), axis=1)

    arrived(recv_o, ro_sem)
    transform = analyse(flat(recv_o), yr, loc_rows, y_it, z_it)
    arrived(recv_s, rs_sem)
    members = flat(recv_s)
    mean = jnp.sum(members, axis=0, keepdims=True) / COUNT
    update = lax.dot_general(
        transform, (members - mean).astype(BF16), (((0,), (0,)), ((), ())),
        preferred_element_type=F32,
    )
    send_r[...] = slabs(mean + update)
    own(send_r, recv_r, rr_sem)
    push(send_r, recv_r, sr_sem, rr_sem, FAR_FIRST)

    across = (((0,), (0,)), ((), ()))
    ones = jnp.ones((COUNT, NS), BF16)
    analysed = lax.dot_general(choose[...], ones, across, preferred_element_type=F32) > 0.5
    to_right.wait_send()
    to_left.wait_send()
    sent(send_s, ss_sem)
    sent(send_o, so_sem)
    arrived(recv_r, rr_sem)
    back = lax.dot_general(
        choose[...], flat(recv_r).astype(BF16), across, preferred_element_type=F32
    )
    out_ref[...] = jnp.where(analysed, back, state_ref[...].astype(F32)).astype(BF16)
    sent(send_r, sr_sem)


def per_device(state, obs_ens, y_obs, obs_rinv, block_list, loc_class, loc_table, patch_active):
    stack = jnp.concatenate(
        [obs_ens, y_obs[None, :], obs_rinv[None, :], jnp.zeros((STACK - MEM - 2, WIDTH), BF16)],
        axis=0,
    )
    vmem = pl.BlockSpec(memory_space=pltpu.VMEM)
    out = pl.pallas_call(
        kernel,
        out_shape=jax.ShapeDtypeStruct((MEM * PAT, NS), BF16),
        in_specs=[vmem] * 5 + [pl.BlockSpec(memory_space=pltpu.SMEM)],
        out_specs=vmem,
        scratch_shapes=[
            pltpu.VMEM((STACK, WIDTH + 2 * HALO), BF16),
            pltpu.VMEM((N, MEM, ROWS), BF16),
            pltpu.VMEM((N, MEM, ROWS), BF16),
            pltpu.VMEM((N, MEM, NS), BF16),
            pltpu.VMEM((N, MEM, NS), BF16),
            pltpu.VMEM((N, MEM, NS), BF16),
            pltpu.VMEM((N, MEM, NS), BF16),
            pltpu.VMEM((COUNT, MEM * PAT), BF16),
            pltpu.VMEM((COUNT, COUNT), F32),
            pltpu.VMEM((COUNT, COUNT), F32),
        ]
        + [pltpu.SemaphoreType.DMA(())] * 6
        + [pltpu.SemaphoreType.DMA((2,))] * 2,
        compiler_params=pltpu.CompilerParams(
            collective_id=0, has_side_effects=True, vmem_limit_bytes=32 * 1024 * 1024
        ),
        cost_estimate=pl.CostEstimate(
            flops=4_000_000_000, bytes_accessed=2_000_000, transcendentals=0
        ),
    )(
        state.reshape(MEM * PAT, NS), stack, block_list, loc_class,
        patch_active[None, :], loc_table,
    )
    return out.reshape(MEM, PAT, NS)


def solution(mesh):
    placed = (
        P("member", "domain", None),
        P("member", "domain"),
        P("domain"),
        P("domain"),
        P("domain", None),
        P("domain", None),
        P(),
        P("domain"),
    )
    return jax.shard_map(
        per_device,
        mesh=mesh,
        in_specs=placed,
        out_specs=P("member", "domain", None),
        check_vma=False,
    )
```

time: 169 us -> 88.6 us (0.52)
  the two profiles are of different devices: /device:TPU:1 before, /device:TPU:12 now
where the time goes in v1:
time: 88.6 us; the launch traced here: 88.3 us
  Pallas kernels  83.1 us (94%)
  local copies, waits for them, and re-layouts  5.05 us (6%)
    pallas_call x1, Pallas kernels, per_device(): pl.pallas_call(kernel, out_shape=jax.ShapeDtypeStruct((MEM * PAT, NS), BF...  83.1 us
    unnamed x19, local copies, waits for them, and re-layouts  4.96 us

profile of v1, /device:TPU:12, one launch (start us, length us, event | category | flops | bytes accessed | tf_op | source)
XLA Modules:
  0.0 88.3 jit_solution(14865134900321468735)
XLA Ops:
  0.0 0.0 copy-start.4
  0.0 0.1 pad.3.clone
  0.1 0.6 copy-done.4
  0.7 0.0 copy-start.5
  0.7 0.7 copy-done.5
  1.4 0.0 copy-start.6
  1.4 0.7 copy-done.6
  2.1 0.0 copy-start.7
  2.1 0.0 copy-start.3
  2.1 0.1 copy.9.list_ref
  2.2 0.6 copy-done.7
  2.8 0.1 copy.10.class_ref
  2.8 0.0 copy-done.3
  2.8 0.0 copy-start.1
  2.8 0.0 copy-start.2
  2.9 0.1 maximum_maximum_fusion.stack_ref
  2.9 0.6 copy-done.1
  3.5 0.0 copy-done.2
  3.5 0.0 copy-start
  3.5 0.9 %copy-done = bf16[8,64,256]{2,1,0:T(8,128)(2,1)S(1)} copy-done((bf16[8,64,256]{2,1,0:T(8,128)(2,1)S(1)}, bf16[8,64,256]{2,1,0:T(8,128)(2,1)}, u32[]{:S(2)}) %copy-start) | copy-done | bytes 262168
  4.5 83.1 %shard_map.82 = bf16[512,256]{1,0:T(8,128)(2,1)S(1)} custom-call(bf16[512,256]{1,0:T(8,128)(2,1)S(1)} %bitcast.4, bf16[16,2048]{1,0:T(8,128)(2,1)S(1)} %maximum_maximum_fusion.stack_ref, s32[64,8]{1,0:T(8,128)S(1)} %copy.9.list_ref, s32[64,8]{1,0:T(8,128)S(1)} %copy.10.class_ref, s32[1,64]{1,0:T(1,128)S(1)} %bitcast.5, f32[8]{0:T(128)S(1)} %copy-done.2), custom_call_target="tpu_custom_call" | custom-call | flops 4000000000 | bytes 2000000 | tf_op jit(solution)/shard_map/pallas_call | solution.py:230
  87.6 0.7 copy.12
  (3 shorter events, 0.0 us)
Async XLA Ops:
  0.0 0.7 copy-start.4
  0.7 0.7 copy-start.5
  1.4 0.7 copy-start.6
  2.1 0.7 copy-start.7
  2.1 0.8 copy-start.3
  2.8 0.7 copy-start.1
  2.8 0.7 copy-start.2
  3.5 0.9 %copy-start = (bf16[8,64,256]{2,1,0:T(8,128)(2,1)S(1)}, bf16[8,64,256]{2,1,0:T(8,128)(2,1)}, u32[]{:S(2)}) copy-start(bf16[8,64,256]{2,1,0:T(8,128)(2,1)} %param.8) | copy-start | bytes 786436

commit v2 on v1

v2 whole, which is shorter than its diff:
```python
import jax
import jax.numpy as jnp
from jax import lax
from jax.experimental import pallas as pl
from jax.experimental.pallas import tpu as pltpu
from jax.sharding import PartitionSpec as P

MESH = pl.DeviceIdType.MESH
F32 = jnp.float32
BF16 = jnp.bfloat16
N = 32
MEM = 8
NS = 256
BROWS = 64
BPP = 8
HB = 6
BLK_DOM = 32
PAT = 64
ROWS = BPP * BROWS
HALO = HB * BROWS
WIDTH = BLK_DOM * BROWS
SIDE = HALO + 256
MAIN = 256 + WIDTH + 256 + 256
TILES = (WIDTH + 2 * HALO) // 128
COUNT = N * MEM
NEWTON = 6
FAR_FIRST = [16] + [s for k in range(15, 0, -1) for s in (k, N - k)]
NT = (((1,), (1,)), ((), ()))
TN = (((0,), (0,)), ((), ()))


def iota(shape, dim):
    return lax.broadcasted_iota(jnp.int32, shape, dim)


def dot(a, b):
    return jnp.dot(a, b, preferred_element_type=F32)


def split(a):
    high = a.astype(BF16)
    return high, (a - high.astype(F32)).astype(BF16)


def dot3(a, b):
    return dot(a[0], b[0]) + (dot(a[0], b[1]) + dot(a[1], b[0]))


def flat(ref):
    value = ref[...].astype(F32)
    return value.reshape(value.shape[0] * value.shape[1], value.shape[2])


def slabs(value):
    return value.reshape(N, MEM, value.shape[-1]).astype(BF16)


def analyse(obs, yr, loc_rows, y_it, z_it):
    mean = jnp.sum(obs, axis=0, keepdims=True) / COUNT
    pert = (obs - mean).astype(BF16)
    weight = yr[1:2] * loc_rows
    weighted = (pert.astype(F32) * weight).astype(BF16)
    gram = lax.dot_general(weighted, pert, (((1,), (1,)), ((), ())), preferred_element_type=F32)
    eye = (iota((COUNT, COUNT), 0) == iota((COUNT, COUNT), 1)).astype(F32)
    system = eye + gram / (COUNT - 1)
    projected = jnp.sum(weighted.astype(F32) * (yr[0:1] - mean), axis=1, keepdims=True)
    squares = jnp.sum(jnp.sum(system * system, axis=0, keepdims=True), axis=1, keepdims=True)
    fro = jnp.sqrt(squares)
    first = system / fro
    half = 1.5 * eye - 0.5 * first
    y_it[...] = dot3(split(first), split(half))
    z_it[...] = half

    def step(_, carry):
        y, z = split(y_it[...]), split(z_it[...])
        middle = split(1.5 * eye - 0.5 * dot3(z, y))
        y_it[...] = dot3(y, middle)
        z_it[...] = dot3(middle, z)
        return carry

    lax.fori_loop(0, NEWTON - 2, step, 0)
    y, z = split(y_it[...]), split(z_it[...])
    last = dot3(split(1.5 * eye - 0.5 * dot3(z, y)), z)
    z = split(last)
    inner = dot3(z, split(jnp.broadcast_to(projected, (COUNT, COUNT))))
    shift = dot3(z, split(inner)) / (fro * (COUNT - 1))
    return (last / jnp.sqrt(fro) + shift).astype(BF16)


def level(group):
    return group // 2 + (N // 2) * (group % 2)


def group_of(lev):
    return 2 * (lev % (N // 2)) + lev // (N // 2)


def ranks(active):
    square = (PAT, PAT)
    upto = (iota(square, 0) <= iota(square, 1)).astype(F32)
    return jnp.where(active > 0.5, dot(active, upto) - 1.0, -1.0)


def kernel(
    state_hbm, obs_hbm, y_hbm, rinv_hbm, list_hbm, class_hbm, active_hbm, table_ref, out_ref,
    state, y_in, rinv_in, list_in, class_in, active_in,
    msg, main, before, after, send_o, recv_o, send_s, relay, recv_s, send_r, recv_r,
    choose, y_it, z_it,
    in_sem, msg_send, msg_recv, so_sem, ro_sem, s1_sem, r1_sem, s2_sem, r2_sem, sr_sem, rr_sem,
):
    group, me = lax.axis_index("domain"), lax.axis_index("member")
    place = level(group)
    served = group_of(me)

    def where_to(dom, mem):
        return {"domain": dom, "member": mem}

    def is_self(dom, mem):
        return (dom == group) & (mem == me)

    inputs = [
        pltpu.make_async_copy(src, dst, in_sem.at[i])
        for i, (src, dst) in enumerate(
            [
                (obs_hbm, msg.at[:, pl.ds(256, WIDTH)]),
                (y_hbm, y_in),
                (rinv_hbm, rinv_in),
                (list_hbm, list_in),
                (class_hbm, class_in),
                (active_hbm, active_in),
                (state_hbm, state),
            ]
        )
    ]
    for copy in inputs:
        copy.start()

    up, down = lax.rem(group + 1, N), lax.rem(group + N - 1, N)
    served_up, served_down = lax.rem(served + 1, N), lax.rem(served + N - 1, N)
    edge = 256 + WIDTH - HALO
    messages = [
        (msg, main, (me, place), (served, group)),
        (msg.at[:, pl.ds(edge, SIDE)], before, (me, level(up)), (served_down, group)),
        (msg.at[:, pl.ds(0, SIDE)], after, (me, level(down)), (served_up, group)),
    ]

    barrier = pltpu.get_barrier_semaphore()
    for k in FAR_FIRST:
        pl.semaphore_signal(
            barrier, inc=1, device_id=where_to(group, lax.rem(me + k, N)), device_id_type=MESH
        )
    for _, _, _, source in messages:

        @pl.when(jnp.logical_not(is_self(*source)))
        def _(source=source):
            pl.semaphore_signal(barrier, inc=1, device_id=where_to(*source), device_id_type=MESH)

    for k in range(1, N):
        pl.semaphore_signal(
            barrier, inc=1, device_id=where_to(lax.rem(group + k, N), me), device_id_type=MESH
        )

    def remote(src, dst, send_sem, recv_sem, target):
        return pltpu.make_async_remote_copy(
            src_ref=src, dst_ref=dst, send_sem=send_sem, recv_sem=recv_sem,
            device_id=where_to(*target), device_id_type=MESH,
        )

    def arrived(dst, recv_sem):
        pltpu.make_async_copy(dst, dst, recv_sem).wait()

    def sent(src, send_sem):
        part = src.at[pl.ds(0, N - 1)]
        pltpu.make_async_copy(part, part, send_sem).wait()

    for copy in inputs[1:6]:
        copy.wait()
    active = jnp.broadcast_to(active_in[...].astype(F32), (8, PAT))
    y_rows, rinv_rows = y_in[...].astype(F32), rinv_in[...].astype(F32)
    msg[:, 0:128] = y_rows[0:8].astype(BF16)
    msg[:, 128:256] = rinv_rows[0:8].astype(BF16)
    msg[:, 256 + WIDTH:384 + WIDTH] = y_rows[8:16].astype(BF16)
    msg[:, 384 + WIDTH:512 + WIDTH] = rinv_rows[8:16].astype(BF16)
    local_ids = (list_in[...] - (group * BLK_DOM - HB)).astype(F32)
    meta = jnp.concatenate([local_ids, class_in[...].astype(F32)], axis=1)
    msg[:, 512 + WIDTH:640 + WIDTH] = meta.astype(BF16)
    msg[:, 640 + WIDTH:768 + WIDTH] = jnp.concatenate([active, active], axis=1).astype(BF16)
    inputs[0].wait()

    big = (COUNT, MEM * PAT)
    rank = ranks(active)[0:1]
    rank = jnp.concatenate([rank] * MEM, axis=1).astype(jnp.int32)
    pick = (rank == iota(big, 0) // MEM) & (iota(big, 1) // PAT == iota(big, 0) % MEM)
    choose[...] = pick.astype(F32).astype(BF16)
    inputs[6].wait()
    send_s[...] = slabs(dot(choose[...], state[...]))

    peers = 2 * (N - 1)
    for _, _, target, _ in messages:
        peers = peers + jnp.where(is_self(*target), 0, 1).astype(jnp.int32)
    pl.semaphore_wait(barrier, peers)

    for i, (src, dst, target, _) in enumerate(messages):

        @pl.when(jnp.logical_not(is_self(*target)))
        def _(src=src, dst=dst, target=target, i=i):
            remote(src, dst, msg_send.at[i], msg_recv.at[i], target).start()

        @pl.when(is_self(*target))
        def _(src=src, dst=dst, i=i):
            pltpu.make_async_copy(src, dst, msg_recv.at[i]).start()

    pltpu.make_async_copy(send_s.at[group], relay.at[group], r1_sem).start()
    for k in range(1, N):
        to = lax.rem(group + k, N)
        remote(send_s.at[to], relay.at[group], s1_sem, r1_sem, (to, me)).start()
    arrived(relay, r1_sem)
    for k in FAR_FIRST:
        to = lax.rem(me + k, N)
        remote(relay.at[group_of(to)], recv_s.at[me], s2_sem, r2_sem, (group, to)).start()
    pltpu.make_async_copy(relay.at[served], recv_s.at[me], r2_sem).start()

    for i, (_, dst, _, _) in enumerate(messages):
        arrived(dst, msg_recv.at[i])
    head = ranks(main[:, 640 + WIDTH:704 + WIDTH].astype(F32))[0:1].astype(jnp.int32)
    meta = main[:, 512 + WIDTH:640 + WIDTH].astype(F32)
    ids, kinds = meta[:, 0:PAT].astype(BF16), meta[:, PAT:2 * PAT].astype(BF16)
    rows = (head == iota((COUNT, PAT), 0) // MEM).astype(F32).astype(BF16)
    listed = lax.dot_general(rows, ids, NT, preferred_element_type=F32).astype(jnp.int32)
    mine = (head == jnp.broadcast_to(group, (8, PAT))).astype(F32).astype(BF16)
    listed_mine = lax.dot_general(mine, ids, NT, preferred_element_type=F32).astype(jnp.int32)
    classes = lax.dot_general(mine, kinds, NT, preferred_element_type=F32).astype(jnp.int32)

    turn = (iota((128, 128), 0) == (iota((128, 128), 1) + BROWS) % 128).astype(F32).astype(BF16)
    half_tile = iota((1, 128), 1) < BROWS

    def both(pieces):
        straight = jnp.concatenate([piece.astype(F32) for piece in pieces], axis=0)
        turned = dot(straight.astype(BF16), turn)
        return jnp.concatenate([straight, turned], axis=0).astype(BF16)

    def gather(table, ids_of, key_of):
        shape = (ids_of.shape[0], table.shape[0])
        tiles = []
        for pair in range(BPP // 2):
            sides = []
            for b in (2 * pair, 2 * pair + 1):
                block = ids_of[:, b:b + 1]
                key = key_of((block + b) & 1, block >> 1)
                hot = (iota(shape, 1) == key).astype(F32).astype(BF16)
                sides.append(dot(hot, table))
            tiles.append(jnp.where(half_tile, sides[0], sides[1]))
        return tiles

    near = HALO // 128
    table = both(
        [before[:, t * 128:(t + 1) * 128] for t in range(near)]
        + [main[:, 256 + t * 128:384 + t * 128] for t in range(WIDTH // 128)]
        + [after[:, 256 + t * 128:384 + t * 128] for t in range(near)]
    )
    member = iota((COUNT, 1), 0) % MEM
    found = gather(table, listed, lambda turned, tile: (turned * TILES + tile) * MEM + member)
    for pair, tile in enumerate(found):
        send_o[:, :, pair * 128:(pair + 1) * 128] = slabs(tile)
    pltpu.make_async_copy(send_o.at[group], recv_o.at[group], ro_sem).start()
    for k in range(1, N):
        to = lax.rem(group + k, N)
        remote(send_o.at[to], recv_o.at[group], so_sem, ro_sem, (to, me)).start()

    values = both(
        [
            piece
            for at in (0, 128)
            for piece in (
                before[:, HALO + at:HALO + at + 128],
                main[:, at:at + 128],
                main[:, 256 + WIDTH + at:384 + WIDTH + at],
                after[:, at:at + 128],
            )
        ]
    )
    which = iota((8, 1), 0) % 2
    yr = jnp.concatenate(
        gather(
            values, listed_mine,
            lambda turned, tile: (turned * 2 + which) * 32 + tile + (8 - near),
        ),
        axis=1,
    )
    weights = jnp.zeros(classes.shape, F32)
    for c in range(8):
        weights = jnp.where(classes == c, table_ref[c], weights)
    lane = iota((1, ROWS), 1) // BROWS
    loc_rows = jnp.zeros((1, ROWS), F32)
    for b in range(BPP):
        loc_rows = jnp.where(lane == b, weights[0:1, b:b + 1], loc_rows)

    arrived(recv_o, ro_sem)
    transform = analyse(flat(recv_o), yr, loc_rows, y_it, z_it)
    arrived(recv_s, r2_sem)
    members = flat(recv_s)
    mean = jnp.sum(members, axis=0, keepdims=True) / COUNT
    update = lax.dot_general(
        transform, (members - mean).astype(BF16), TN, preferred_element_type=F32
    )
    send_r[...] = slabs(mean + update)
    for k in FAR_FIRST:
        to = lax.rem(me + k, N)
        remote(send_r.at[to], recv_r.at[group], sr_sem, rr_sem, (served, to)).start()
    home = served == group
    last = remote(send_r.at[me], recv_r.at[group], sr_sem, rr_sem, (served, me))

    @pl.when(jnp.logical_not(home))
    def _():
        last.start()

    @pl.when(home)
    def _():
        pltpu.make_async_copy(send_r.at[me], recv_r.at[group], rr_sem).start()

    ones = jnp.ones((COUNT, NS), BF16)
    analysed = lax.dot_general(choose[...], ones, TN, preferred_element_type=F32) > 0.5
    for i, (src, _, target, _) in enumerate(messages):

        @pl.when(jnp.logical_not(is_self(*target)))
        def _(src=src, i=i):
            pltpu.make_async_copy(src, src, msg_send.at[i]).wait()

    sent(send_s, s1_sem)
    sent(relay, s2_sem)
    sent(send_o, so_sem)
    arrived(recv_r, rr_sem)
    back = lax.dot_general(
        choose[...], flat(recv_r).astype(BF16), TN, preferred_element_type=F32
    )
    out_ref[...] = jnp.where(analysed, back, state[...].astype(F32)).astype(BF16)
    sent(send_r, sr_sem)

    @pl.when(jnp.logical_not(home))
    def _():
        one = send_r.at[0]
        pltpu.make_async_copy(one, one, sr_sem).wait()


def per_device(state, obs_ens, y_obs, obs_rinv, block_list, loc_class, loc_table, patch_active):
    hbm = pl.BlockSpec(memory_space=pltpu.HBM)
    slab = pltpu.VMEM((N, MEM, NS), BF16)
    wide = pltpu.VMEM((N, MEM, ROWS), BF16)
    out = pl.pallas_call(
        kernel,
        out_shape=jax.ShapeDtypeStruct((MEM * PAT, NS), BF16),
        in_specs=[hbm] * 7 + [pl.BlockSpec(memory_space=pltpu.SMEM)],
        out_specs=pl.BlockSpec(memory_space=pltpu.VMEM),
        scratch_shapes=[
            pltpu.VMEM((MEM * PAT, NS), BF16),
            pltpu.VMEM((16, 128), BF16),
            pltpu.VMEM((16, 128), BF16),
            pltpu.VMEM((BPP, PAT), jnp.int32),
            pltpu.VMEM((BPP, PAT), jnp.int32),
            pltpu.VMEM((1, PAT), jnp.int32),
            pltpu.VMEM((MEM, MAIN), BF16),
            pltpu.VMEM((MEM, MAIN), BF16),
            pltpu.VMEM((MEM, SIDE), BF16),
            pltpu.VMEM((MEM, SIDE), BF16),
            wide, wide, slab, slab, slab, slab, slab,
            pltpu.VMEM((COUNT, MEM * PAT), BF16),
            pltpu.VMEM((COUNT, COUNT), F32),
            pltpu.VMEM((COUNT, COUNT), F32),
            pltpu.SemaphoreType.DMA((7,)),
            pltpu.SemaphoreType.DMA((3,)),
            pltpu.SemaphoreType.DMA((3,)),
        ]
        + [pltpu.SemaphoreType.DMA(())] * 8,
        compiler_params=pltpu.CompilerParams(
            collective_id=0, has_side_effects=True, vmem_limit_bytes=56 * 1024 * 1024
        ),
        cost_estimate=pl.CostEstimate(
            flops=4_000_000_000, bytes_accessed=2_000_000, transcendentals=0
        ),
    )(
        state.reshape(MEM * PAT, NS), obs_ens, y_obs.reshape(16, 128), obs_rinv.reshape(16, 128),
        block_list.T, loc_class.T, patch_active[None, :], loc_table,
    )
    return out.reshape(MEM, PAT, NS)


def solution(mesh):
    placed = (
        P("member", "domain", None),
        P("member", "domain"),
        P("domain"),
        P("domain"),
        P("domain", None),
        P("domain", None),
        P(),
        P("domain"),
    )
    return jax.shard_map(
        per_device,
        mesh=mesh,
        in_specs=placed,
        out_specs=P("member", "domain", None),
        check_vma=False,
    )
```

time: 88.6 us -> 84.4 us (0.953)
  the two profiles are of different devices: /device:TPU:12 before, /device:TPU:3 now
where the time goes in v2:
time: 84.4 us; the launch traced here: 84.2 us
  Pallas kernels  82.6 us (98%)
  local copies, waits for them, and re-layouts  1.67 us (2%)
    pallas_call x1, Pallas kernels, per_device(): pl.pallas_call(kernel, out_shape=jax.ShapeDtypeStruct((MEM * PAT, NS), BF...  82.6 us

profile of v2, /device:TPU:3, one launch (start us, length us, event | category | flops | bytes accessed | tf_op | source)
XLA Modules:
  0.0 84.2 jit_solution(11559036612452186338)
XLA Ops:
  0.0 82.6 %shard_map.82 = bf16[512,256]{1,0:T(8,128)(2,1)} custom-call(bf16[512,256]{1,0:T(8,128)(2,1)} %bitcast.8, bf16[8,2048]{1,0:T(8,128)(2,1)} %obs_hbm.1, bf16[16,128]{1,0:T(8,128)(2,1)} %bitcast.9, bf16[16,128]{1,0:T(8,128)(2,1)} %bitcast.10, s32[8,64]{1,0:T(8,128)} %bitcast.11, s32[8,64]{1,0:T(8,128)} %bitcast.12, s32[1,64]{1,0:T(1,128)} %bitcast.13, f32[8]{0:T(128)} %table_ref.1), custom_call_target="tpu_custom_call" | custom-call | flops 4000000000 | bytes 2000000 | tf_op jit(solution)/shard_map/pallas_call | solution.py:349
  82.6 1.7 %copy.10 = bf16[8,64,256]{2,1,0:T(8,128)(2,1)} copy(bf16[8,64,256]{2,1,0:T(8,128)(2,1)} %bitcast.7) | data formatting | bytes 524288

commit v3 on v2

v3 whole, which is shorter than its diff:
```python
import jax
import jax.numpy as jnp
from jax import lax
from jax.experimental import pallas as pl
from jax.experimental.pallas import tpu as pltpu
from jax.sharding import PartitionSpec as P

MESH = pl.DeviceIdType.MESH
F32 = jnp.float32
BF16 = jnp.bfloat16
N = 32
MEM = 8
NS = 256
BROWS = 64
BPP = 8
HB = 6
BLK_DOM = 32
PAT = 64
ROWS = BPP * BROWS
HALO = HB * BROWS
WIDTH = BLK_DOM * BROWS
COUNT = N * MEM
NEWTON = 6
CUT = BROWS // N
SLAB = 128
EDGE = CUT * HB
OWN = CUT * BLK_DOM
Y_AT = OWN + 2 * EDGE
R_AT, ID_AT, KIND_AT = Y_AT + 1, Y_AT + 2, Y_AT + 3
FAR_FIRST = [16] + [s for k in range(15, 0, -1) for s in (k, N - k)]
NT = (((1,), (1,)), ((), ()))
TN = (((0,), (0,)), ((), ()))


def iota(shape, dim):
    return lax.broadcasted_iota(jnp.int32, shape, dim)


def dot(a, b):
    return jnp.dot(a, b, preferred_element_type=F32)


def split(a):
    high = a.astype(BF16)
    return high, (a - high.astype(F32)).astype(BF16)


def dot_dims(a, b, dims):
    return lax.dot_general(a, b, dims, preferred_element_type=F32)


def dot3(a, b, dims=(((1,), (0,)), ((), ()))):
    return dot_dims(a[0], b[0], dims) + (dot_dims(a[0], b[1], dims) + dot_dims(a[1], b[0], dims))


def one_hot(condition):
    return condition.astype(F32).astype(BF16)


def flat(ref):
    value = ref[...].astype(F32)
    return value.reshape(value.shape[0] * value.shape[1], value.shape[2])


def slabs(value):
    return value.reshape(N, MEM, value.shape[-1]).astype(BF16)


def analyse(rows, table_ref, y_it, z_it):
    obs = rows[:, :COUNT]
    mean = dot(obs.astype(BF16), jnp.ones((COUNT, COUNT), BF16)) / COUNT
    pert = (obs - mean).astype(BF16)
    kind = rows[:, COUNT + KIND_AT:COUNT + KIND_AT + 1]
    local = jnp.zeros(kind.shape, F32)
    for c in range(8):
        local = jnp.where(kind == c, table_ref[c], local)
    weight = rows[:, COUNT + R_AT:COUNT + R_AT + 1] * local
    weighted = (pert.astype(F32) * weight).astype(BF16)
    gram = dot_dims(weighted, pert, TN)
    eye = (iota((COUNT, COUNT), 0) == iota((COUNT, COUNT), 1)).astype(F32)
    system = eye + gram / (COUNT - 1)
    innovation = rows[:, COUNT + Y_AT:COUNT + Y_AT + 1] - mean
    projected = jnp.sum(weighted.astype(F32) * innovation, axis=0, keepdims=True)
    squares = jnp.sum(jnp.sum(system * system, axis=0, keepdims=True), axis=1, keepdims=True)
    fro = jnp.sqrt(squares)
    first = system / fro
    half = 1.5 * eye - 0.5 * first
    y_it[...] = dot3(split(first), split(half))
    z_it[...] = half

    def step(_, carry):
        y, z = split(y_it[...]), split(z_it[...])
        middle = split(1.5 * eye - 0.5 * dot3(z, y))
        y_it[...] = dot3(y, middle)
        z_it[...] = dot3(middle, z)
        return carry

    lax.fori_loop(0, NEWTON - 2, step, 0)
    y, z = split(y_it[...]), split(z_it[...])
    last = dot3(split(1.5 * eye - 0.5 * dot3(z, y)), z)
    z = split(last)
    inner = dot3(z, split(jnp.broadcast_to(projected, (COUNT, COUNT))), NT)
    shift = dot3(z, split(inner)) / (fro * (COUNT - 1))
    return (last / jnp.sqrt(fro) + shift).astype(BF16)


def level(group):
    return group // 2 + (N // 2) * (group % 2)


def group_of(lev):
    return 2 * (lev % (N // 2)) + lev // (N // 2)


def ranks(active):
    square = (PAT, PAT)
    upto = (iota(square, 0) <= iota(square, 1)).astype(F32)
    return jnp.where(active > 0.5, dot(active, upto) - 1.0, -1.0)


def kernel(
    state_hbm, obs_hbm, y_hbm, rinv_hbm, list_hbm, class_hbm, active_hbm, table_ref, out_ref,
    state, obs_in, y_in, rinv_in, list_in, class_in, active_in,
    send1, relay, send2, recv2, recv_s, send3, recv3, send_r, recv_r, choose, y_it, z_it,
    in_sem, s1_sem, r1_sem, s2_sem, r2_sem, ss_sem, rs_sem, s3_sem, r3_sem, sr_sem, rr_sem,
):
    group, me = lax.axis_index("domain"), lax.axis_index("member")
    served = group_of(me)

    inputs = [
        pltpu.make_async_copy(src, dst, in_sem.at[i])
        for i, (src, dst) in enumerate(
            [
                (active_hbm, active_in),
                (list_hbm, list_in),
                (class_hbm, class_in),
                (y_hbm, y_in),
                (rinv_hbm, rinv_in),
                (obs_hbm, obs_in),
                (state_hbm, state),
            ]
        )
    ]
    for copy in inputs:
        copy.start()

    barrier = pltpu.get_barrier_semaphore()
    for k in FAR_FIRST:
        to = {"domain": group, "member": lax.rem(me + k, N)}
        pl.semaphore_signal(barrier, inc=1, device_id=to, device_id_type=MESH)
    for k in range(1, N):
        to = {"domain": lax.rem(group + k, N), "member": me}
        pl.semaphore_signal(barrier, inc=1, device_id=to, device_id_type=MESH)

    def remote(src, dst, send_sem, recv_sem, dom, mem):
        return pltpu.make_async_remote_copy(
            src_ref=src, dst_ref=dst, send_sem=send_sem, recv_sem=recv_sem,
            device_id={"domain": dom, "member": mem}, device_id_type=MESH,
        )

    def arrived(dst, recv_sem):
        pltpu.make_async_copy(dst, dst, recv_sem).wait()

    def sent(src, send_sem):
        part = src.at[pl.ds(0, N - 1)]
        pltpu.make_async_copy(part, part, send_sem).wait()

    def plane(src, dst, send_sem, recv_sem):
        pltpu.make_async_copy(src.at[group], dst.at[group], recv_sem).start()
        for k in range(1, N):
            to = lax.rem(group + k, N)
            remote(src.at[to], dst.at[group], send_sem, recv_sem, to, me).start()

    def column(src_at, dst, send_sem, recv_sem):
        for k in FAR_FIRST:
            to = lax.rem(me + k, N)
            remote(src_at(group_of(to)), dst.at[me], send_sem, recv_sem, group, to).start()
        pltpu.make_async_copy(src_at(served), dst.at[me], recv_sem).start()

    for copy in inputs[:6]:
        copy.wait()
    active = jnp.broadcast_to(active_in[...].astype(F32), (8, PAT))
    rank = ranks(active)
    mine = rank == jnp.broadcast_to(me, (8, PAT)).astype(F32)
    local_ids = (list_in[...] - (group * BLK_DOM - HB)).astype(F32)
    ids = jnp.sum(jnp.where(mine, local_ids, 0.0), axis=1, keepdims=True)
    kinds = jnp.sum(jnp.where(mine, class_in[...].astype(F32), 0.0), axis=1, keepdims=True)

    square = (COUNT, 128)
    row, lane = iota(square, 0), iota(square, 1)
    member = row % MEM
    ours = (lane % BROWS) // CUT == row // MEM
    spot = (lane // BROWS) * CUT + lane % CUT
    obs = obs_in[...].astype(F32)
    parts = []
    for t in range(WIDTH // 128):
        tile = jnp.concatenate([obs[:, t * 128:(t + 1) * 128]] * N, axis=0)
        parts.append(jnp.where(ours, tile, 0.0).astype(BF16))
    narrow = (COUNT, 16)
    tile_of = one_hot(iota(narrow, 1) == 2 * (me % 8) + (iota(narrow, 0) % MEM) // 4)
    for values in (y_in, rinv_in):
        tile = dot(tile_of, values[...])
        parts.append(jnp.where(ours & (spot == member % 4), tile, 0.0).astype(BF16))
    tall = (WIDTH, SLAB)
    at = iota(tall, 0)
    goal = (at // 128) * (2 * CUT) + ((at % 128) // BROWS) * CUT + at % CUT
    place = [one_hot(iota(tall, 1) == goal)] + [one_hot(lane[:128] == a) for a in (Y_AT, R_AT)]
    packed = dot(jnp.concatenate(parts, axis=1), jnp.concatenate(place, axis=0))
    packed = jnp.where(lane == ID_AT, jnp.concatenate([ids] * N, axis=0), packed)
    packed = jnp.where(lane == KIND_AT, jnp.concatenate([kinds] * N, axis=0), packed)
    send1[:, :, 0:SLAB] = slabs(packed)

    big = (COUNT, MEM * PAT)
    wide_rank = jnp.concatenate([rank[0:1]] * MEM, axis=1).astype(jnp.int32)
    choose[...] = one_hot(
        (wide_rank == iota(big, 0) // MEM) & (iota(big, 1) // PAT == iota(big, 0) % MEM)
    )
    inputs[6].wait()
    send1[:, :, SLAB:SLAB + NS] = slabs(dot(choose[...], state[...]))

    square = (SLAB, SLAB)
    source, goal = iota(square, 0), iota(square, 1)
    plain = source == goal
    value = plain & ((goal == Y_AT) | (goal == R_AT))
    turn = me // 8
    mix = jnp.concatenate(
        [
            one_hot(
                (plain & ((goal < OWN) | (goal == ID_AT) | (goal == KIND_AT)))
                | (value & (turn == 0))
            ),
            one_hot(
                ((goal >= OWN) & (goal < OWN + EDGE) & (source == goal - EDGE))
                | (value & (turn == 1))
            ),
            one_hot(
                ((goal >= OWN + EDGE) & (goal < Y_AT) & (source == goal - OWN - EDGE))
                | (value & (turn == 2))
            ),
        ],
        axis=0,
    )

    pl.semaphore_wait(barrier, 2 * (N - 1))
    plane(send1, relay, s1_sem, r1_sem)
    arrived(relay, r1_sem)
    here = flat(relay.at[:, :, pl.ds(0, SLAB)])
    lower = jnp.concatenate([here[COUNT - MEM:], here[:COUNT - MEM]], axis=0)
    upper = jnp.concatenate([here[MEM:], here[:MEM]], axis=0)
    send2[...] = slabs(dot(jnp.concatenate([here, lower, upper], axis=1).astype(BF16), mix))
    column(lambda g: send2.at[g], recv2, s2_sem, r2_sem)
    column(lambda g: relay.at[g, :, pl.ds(SLAB, NS)], recv_s, ss_sem, rs_sem)

    arrived(recv2, r2_sem)
    held = flat(recv2)
    ids = held[:, ID_AT:ID_AT + 1].astype(jnp.int32)
    kinds = held[:, KIND_AT:KIND_AT + 1]
    held = held.astype(BF16)
    low, high = ids < HB, ids >= HB + BLK_DOM
    inner = CUT * (ids - HB)
    column_at = jnp.where(low, OWN + CUT * ids, jnp.where(high, inner + EDGE, inner))
    value_at = jnp.where(
        low, OWN + inner + OWN, jnp.where(high, inner - OWN + 2 * OWN, inner)
    )
    for cut in range(CUT):
        hot = one_hot(iota((COUNT, SLAB), 1) == column_at + cut)
        send3[:, cut, :, 0:COUNT] = slabs(dot_dims(hot, held, NT))
        hot = one_hot(iota((COUNT, COUNT), 1) == value_at + cut)
        values = jnp.where(lane == KIND_AT, kinds, dot(hot, held))
        send3[:, cut, :, COUNT:COUNT + SLAB] = slabs(values)
    plane(send3, recv3, s3_sem, r3_sem)

    arrived(recv3, r3_sem)
    rows = recv3[...].astype(F32).reshape(ROWS, COUNT + SLAB)
    transform = analyse(rows, table_ref, y_it, z_it)
    arrived(recv_s, rs_sem)
    members = flat(recv_s)
    mean = jnp.sum(members, axis=0, keepdims=True) / COUNT
    update = dot_dims(transform, (members - mean).astype(BF16), TN)
    send_r[...] = slabs(mean + update)
    for k in FAR_FIRST:
        to = lax.rem(me + k, N)
        remote(send_r.at[to], recv_r.at[group], sr_sem, rr_sem, served, to).start()
    home = served == group

    @pl.when(jnp.logical_not(home))
    def _():
        remote(send_r.at[me], recv_r.at[group], sr_sem, rr_sem, served, me).start()

    @pl.when(home)
    def _():
        pltpu.make_async_copy(send_r.at[me], recv_r.at[group], rr_sem).start()

    ones = jnp.ones((COUNT, NS), BF16)
    analysed = dot_dims(choose[...], ones, TN) > 0.5
    sent(send1, s1_sem)
    sent(send2, s2_sem)
    sent(recv_s, ss_sem)
    sent(send3, s3_sem)
    arrived(recv_r, rr_sem)
    back = dot_dims(choose[...], flat(recv_r).astype(BF16), TN)
    out_ref[...] = jnp.where(analysed, back, state[...].astype(F32)).astype(BF16)
    sent(send_r, sr_sem)

    @pl.when(jnp.logical_not(home))
    def _():
        one = send_r.at[0]
        pltpu.make_async_copy(one, one, sr_sem).wait()


def per_device(state, obs_ens, y_obs, obs_rinv, block_list, loc_class, loc_table, patch_active):
    hbm = pl.BlockSpec(memory_space=pltpu.HBM)
    slab = pltpu.VMEM((N, MEM, NS), BF16)
    out = pl.pallas_call(
        kernel,
        out_shape=jax.ShapeDtypeStruct((MEM * PAT, NS), BF16),
        in_specs=[hbm] * 7 + [pl.BlockSpec(memory_space=pltpu.SMEM)],
        out_specs=pl.BlockSpec(memory_space=pltpu.VMEM),
        scratch_shapes=[
            pltpu.VMEM((MEM * PAT, NS), BF16),
            pltpu.VMEM((MEM, WIDTH), BF16),
            pltpu.VMEM((16, 128), BF16),
            pltpu.VMEM((16, 128), BF16),
            pltpu.VMEM((BPP, PAT), jnp.int32),
            pltpu.VMEM((BPP, PAT), jnp.int32),
            pltpu.VMEM((1, PAT), jnp.int32),
            pltpu.VMEM((N, MEM, SLAB + NS), BF16),
            pltpu.VMEM((N, MEM, SLAB + NS), BF16),
            pltpu.VMEM((N, MEM, SLAB), BF16),
            pltpu.VMEM((N, MEM, SLAB), BF16),
            slab,
            pltpu.VMEM((N, CUT, MEM, COUNT + SLAB), BF16),
            pltpu.VMEM((N, CUT, MEM, COUNT + SLAB), BF16),
            slab,
            slab,
            pltpu.VMEM((COUNT, MEM * PAT), BF16),
            pltpu.VMEM((COUNT, COUNT), F32),
            pltpu.VMEM((COUNT, COUNT), F32),
            pltpu.SemaphoreType.DMA((7,)),
        ]
        + [pltpu.SemaphoreType.DMA(())] * 10,
        compiler_params=pltpu.CompilerParams(
            collective_id=0, has_side_effects=True, vmem_limit_bytes=56 * 1024 * 1024
        ),
        cost_estimate=pl.CostEstimate(
            flops=4_000_000_000, bytes_accessed=2_000_000, transcendentals=0
        ),
    )(
        state.reshape(MEM * PAT, NS), obs_ens, y_obs.reshape(16, 128), obs_rinv.reshape(16, 128),
        block_list.T, loc_class.T, patch_active[None, :], loc_table,
    )
    return out.reshape(MEM, PAT, NS)


def solution(mesh):
    placed = (
        P("member", "domain", None),
        P("member", "domain"),
        P("domain"),
        P("domain"),
        P("domain", None),
        P("domain", None),
        P(),
        P("domain"),
    )
    return jax.shard_map(
        per_device,
        mesh=mesh,
        in_specs=placed,
        out_specs=P("member", "domain", None),
        check_vma=False,
    )
```

time: 84.4 us -> 82 us (0.972)
  Pallas kernels: 82.6 us -> 80.1 us
    pallas_call x1, Pallas kernels: 82.6 us -> 80.1 us  [per_device(): pl.pallas_call(kernel, out_shape=jax.ShapeDtypeStruct((MEM * PAT, NS), BF...]
where the time goes in v3:
time: 82 us; the launch traced here: 81.8 us
  Pallas kernels  80.1 us (98%)
  local copies, waits for them, and re-layouts  1.67 us (2%)
    pallas_call x1, Pallas kernels, per_device(): pl.pallas_call(kernel, out_shape=jax.ShapeDtypeStruct((MEM * PAT, NS), BF...  80.1 us
    unnamed x1, local copies, waits for them, and re-layouts  1.67 us

profile of v3, /device:TPU:3, one launch (start us, length us, event | category | flops | bytes accessed | tf_op | source)
XLA Modules:
  0.0 81.8 jit_solution(5550093611000690356)
XLA Ops:
  0.0 80.1 %shard_map.82 = bf16[512,256]{1,0:T(8,128)(2,1)} custom-call(bf16[512,256]{1,0:T(8,128)(2,1)} %bitcast.8, bf16[8,2048]{1,0:T(8,128)(2,1)} %obs_hbm.1, bf16[16,128]{1,0:T(8,128)(2,1)} %bitcast.9, bf16[16,128]{1,0:T(8,128)(2,1)} %bitcast.10, s32[8,64]{1,0:T(8,128)} %bitcast.11, s32[8,64]{1,0:T(8,128)} %bitcast.12, s32[1,64]{1,0:T(1,128)} %bitcast.13, f32[8]{0:T(128)} %table_ref.1), custom_call_target="tpu_custom_call" | custom-call | flops 4000000000 | bytes 2000000 | tf_op jit(solution)/shard_map/pallas_call | solution.py:314
  80.2 1.7 %copy.10 = bf16[8,64,256]{2,1,0:T(8,128)(2,1)} copy(bf16[8,64,256]{2,1,0:T(8,128)(2,1)} %bitcast.7) | data formatting | bytes 524288

commit v4 on v3

--- a/solution.py
+++ b/solution.py
@@ -27,7 +27,10 @@
 OWN = CUT * BLK_DOM
 Y_AT = OWN + 2 * EDGE
 R_AT, ID_AT, KIND_AT = Y_AT + 1, Y_AT + 2, Y_AT + 3
+SIDE = 16
 FAR_FIRST = [16] + [s for k in range(15, 0, -1) for s in (k, N - k)]
+STEPS = (0, 1, 2, 1)
+PLANE = sorted(range(1, N), key=lambda k: -STEPS[k // 8] - STEPS[k % 8 // 2])
 NT = (((1,), (1,)), ((), ()))
 TN = (((0,), (0,)), ((), ()))
 
@@ -66,20 +69,22 @@
     return value.reshape(N, MEM, value.shape[-1]).astype(BF16)
 
 
-def analyse(rows, table_ref, y_it, z_it):
-    obs = rows[:, :COUNT]
+def analyse(obs, values, table, y_it, z_it):
+    def column_of(at, step):
+        return jnp.concatenate([values[:, at + step * k:at + step * k + 1] for k in range(CUT)], 0)
+
     mean = dot(obs.astype(BF16), jnp.ones((COUNT, COUNT), BF16)) / COUNT
     pert = (obs - mean).astype(BF16)
-    kind = rows[:, COUNT + KIND_AT:COUNT + KIND_AT + 1]
+    kind = column_of(KIND_AT, 0)
     local = jnp.zeros(kind.shape, F32)
     for c in range(8):
-        local = jnp.where(kind == c, table_ref[c], local)
-    weight = rows[:, COUNT + R_AT:COUNT + R_AT + 1] * local
+        local = jnp.where(kind == c, table[:, c:c + 1], local)
+    weight = column_of(R_AT, SIDE) * local
     weighted = (pert.astype(F32) * weight).astype(BF16)
     gram = dot_dims(weighted, pert, TN)
     eye = (iota((COUNT, COUNT), 0) == iota((COUNT, COUNT), 1)).astype(F32)
     system = eye + gram / (COUNT - 1)
-    innovation = rows[:, COUNT + Y_AT:COUNT + Y_AT + 1] - mean
+    innovation = column_of(Y_AT, SIDE) - mean
     projected = jnp.sum(weighted.astype(F32) * innovation, axis=0, keepdims=True)
     squares = jnp.sum(jnp.sum(system * system, axis=0, keepdims=True), axis=1, keepdims=True)
     fro = jnp.sqrt(squares)
@@ -119,10 +124,10 @@
 
 
 def kernel(
-    state_hbm, obs_hbm, y_hbm, rinv_hbm, list_hbm, class_hbm, active_hbm, table_ref, out_ref,
-    state, obs_in, y_in, rinv_in, list_in, class_in, active_in,
-    send1, relay, send2, recv2, recv_s, send3, recv3, send_r, recv_r, choose, y_it, z_it,
-    in_sem, s1_sem, r1_sem, s2_sem, r2_sem, ss_sem, rs_sem, s3_sem, r3_sem, sr_sem, rr_sem,
+    state_hbm, obs_hbm, y_hbm, rinv_hbm, list_hbm, class_hbm, active_hbm, table_hbm, out_ref,
+    state, obs_in, y_in, rinv_in, list_in, class_in, active_in, table_in,
+    send1, relay, send_s, relay_s, send2, recv2, recv_s, send3, recv3, send_r, recv_r, choose, y_it, z_it,
+    in_sem, s1_sem, r1_sem, sp_sem, rp_sem, s2_sem, r2_sem, ss_sem, rs_sem, s3_sem, r3_sem, sr_sem, rr_sem,
 ):
     group, me = lax.axis_index("domain"), lax.axis_index("member")
     served = group_of(me)
@@ -138,6 +143,7 @@
                 (rinv_hbm, rinv_in),
                 (obs_hbm, obs_in),
                 (state_hbm, state),
+                (table_hbm, table_in),
             ]
         )
     ]
@@ -167,7 +173,7 @@
 
     def plane(src, dst, send_sem, recv_sem):
         pltpu.make_async_copy(src.at[group], dst.at[group], recv_sem).start()
-        for k in range(1, N):
+        for k in PLANE:
             to = lax.rem(group + k, N)
             remote(src.at[to], dst.at[group], send_sem, recv_sem, to, me).start()
 
@@ -208,7 +214,7 @@
     packed = dot(jnp.concatenate(parts, axis=1), jnp.concatenate(place, axis=0))
     packed = jnp.where(lane == ID_AT, jnp.concatenate([ids] * N, axis=0), packed)
     packed = jnp.where(lane == KIND_AT, jnp.concatenate([kinds] * N, axis=0), packed)
-    send1[:, :, 0:SLAB] = slabs(packed)
+    send1[...] = slabs(packed)
 
     big = (COUNT, MEM * PAT)
     wide_rank = jnp.concatenate([rank[0:1]] * MEM, axis=1).astype(jnp.int32)
@@ -216,7 +222,8 @@
         (wide_rank == iota(big, 0) // MEM) & (iota(big, 1) // PAT == iota(big, 0) % MEM)
     )
     inputs[6].wait()
-    send1[:, :, SLAB:SLAB + NS] = slabs(dot(choose[...], state[...]))
+    inputs[7].wait()
+    send_s[...] = slabs(dot(choose[...], state[...]))
 
     square = (SLAB, SLAB)
     source, goal = iota(square, 0), iota(square, 1)
@@ -243,13 +250,15 @@
 
     pl.semaphore_wait(barrier, 2 * (N - 1))
     plane(send1, relay, s1_sem, r1_sem)
+    plane(send_s, relay_s, sp_sem, rp_sem)
     arrived(relay, r1_sem)
-    here = flat(relay.at[:, :, pl.ds(0, SLAB)])
+    here = flat(relay)
     lower = jnp.concatenate([here[COUNT - MEM:], here[:COUNT - MEM]], axis=0)
     upper = jnp.concatenate([here[MEM:], here[:MEM]], axis=0)
     send2[...] = slabs(dot(jnp.concatenate([here, lower, upper], axis=1).astype(BF16), mix))
     column(lambda g: send2.at[g], recv2, s2_sem, r2_sem)
-    column(lambda g: relay.at[g, :, pl.ds(SLAB, NS)], recv_s, ss_sem, rs_sem)
+    arrived(relay_s, rp_sem)
+    column(lambda g: relay_s.at[g], recv_s, ss_sem, rs_sem)
 
     arrived(recv2, r2_sem)
     held = flat(recv2)
@@ -262,17 +271,31 @@
     value_at = jnp.where(
         low, OWN + inner + OWN, jnp.where(high, inner - OWN + 2 * OWN, inner)
     )
+    values = []
     for cut in range(CUT):
         hot = one_hot(iota((COUNT, SLAB), 1) == column_at + cut)
-        send3[:, cut, :, 0:COUNT] = slabs(dot_dims(hot, held, NT))
+        picked = slabs(dot_dims(hot, held, NT))
+        send3[:, 2 * cut] = picked[:, :, 0:128]
+        send3[:, 2 * cut + 1] = picked[:, :, 128:256]
         hot = one_hot(iota((COUNT, COUNT), 1) == value_at + cut)
-        values = jnp.where(lane == KIND_AT, kinds, dot(hot, held))
-        send3[:, cut, :, COUNT:COUNT + SLAB] = slabs(values)
+        values.append(dot(hot, held))
+    turned = dot(values[1].astype(BF16), one_hot(source == goal - SIDE))
+    values = jnp.where(lane < Y_AT + SIDE, values[0], turned)
+    send3[:, 2 * CUT] = slabs(jnp.where(lane == KIND_AT, kinds, values))
     plane(send3, recv3, s3_sem, r3_sem)
 
     arrived(recv3, r3_sem)
-    rows = recv3[...].astype(F32).reshape(ROWS, COUNT + SLAB)
-    transform = analyse(rows, table_ref, y_it, z_it)
+    def part(i):
+        return recv3[:, i].astype(F32).reshape(COUNT, SLAB)
+
+    obs = jnp.concatenate(
+        [
+            jnp.concatenate([part(2 * cut) for cut in range(CUT)], axis=0),
+            jnp.concatenate([part(2 * cut + 1) for cut in range(CUT)], axis=0),
+        ],
+        axis=1,
+    )
+    transform = analyse(obs, part(2 * CUT), table_in[...], y_it, z_it)
     arrived(recv_s, rs_sem)
     members = flat(recv_s)
     mean = jnp.sum(members, axis=0, keepdims=True) / COUNT
@@ -294,8 +317,9 @@
     ones = jnp.ones((COUNT, NS), BF16)
     analysed = dot_dims(choose[...], ones, TN) > 0.5
     sent(send1, s1_sem)
+    sent(send_s, sp_sem)
     sent(send2, s2_sem)
-    sent(recv_s, ss_sem)
+    sent(relay_s, ss_sem)
     sent(send3, s3_sem)
     arrived(recv_r, rr_sem)
     back = dot_dims(choose[...], flat(recv_r).astype(BF16), TN)
@@ -314,7 +338,7 @@
     out = pl.pallas_call(
         kernel,
         out_shape=jax.ShapeDtypeStruct((MEM * PAT, NS), BF16),
-        in_specs=[hbm] * 7 + [pl.BlockSpec(memory_space=pltpu.SMEM)],
+        in_specs=[hbm] * 8,
         out_specs=pl.BlockSpec(memory_space=pltpu.VMEM),
         scratch_shapes=[
             pltpu.VMEM((MEM * PAT, NS), BF16),
@@ -324,30 +348,39 @@
             pltpu.VMEM((BPP, PAT), jnp.int32),
             pltpu.VMEM((BPP, PAT), jnp.int32),
             pltpu.VMEM((1, PAT), jnp.int32),
-            pltpu.VMEM((N, MEM, SLAB + NS), BF16),
-            pltpu.VMEM((N, MEM, SLAB + NS), BF16),
+            pltpu.VMEM((1, 8), F32),
             pltpu.VMEM((N, MEM, SLAB), BF16),
             pltpu.VMEM((N, MEM, SLAB), BF16),
             slab,
-            pltpu.VMEM((N, CUT, MEM, COUNT + SLAB), BF16),
-            pltpu.VMEM((N, CUT, MEM, COUNT + SLAB), BF16),
+            slab,
+            pltpu.VMEM((N, MEM, SLAB), BF16),
+            pltpu.VMEM((N, MEM, SLAB), BF16),
+            slab,
+            pltpu.VMEM((N, 2 * CUT + 1, MEM, SLAB), BF16),
+            pltpu.VMEM((N, 2 * CUT + 1, MEM, SLAB), BF16),
             slab,
             slab,
             pltpu.VMEM((COUNT, MEM * PAT), BF16),
             pltpu.VMEM((COUNT, COUNT), F32),
             pltpu.VMEM((COUNT, COUNT), F32),
-            pltpu.SemaphoreType.DMA((7,)),
+            pltpu.SemaphoreType.DMA((8,)),
         ]
-        + [pltpu.SemaphoreType.DMA(())] * 10,
+        + [pltpu.SemaphoreType.DMA(())] * 12,
         compiler_params=pltpu.CompilerParams(
-            collective_id=0, has_side_effects=True, vmem_limit_bytes=56 * 1024 * 1024
+            collective_id=0, has_side_effects=True, vmem_limit_bytes=32 * 1024 * 1024
         ),
         cost_estimate=pl.CostEstimate(
             flops=4_000_000_000, bytes_accessed=2_000_000, transcendentals=0
         ),
     )(
-        state.reshape(MEM * PAT, NS), obs_ens, y_obs.reshape(16, 128), obs_rinv.reshape(16, 128),
-        block_list.T, loc_class.T, patch_active[None, :], loc_table,
+        *[
+            pltpu.with_memory_space_constraint(x, pltpu.HBM)
+            for x in (
+                state.reshape(MEM * PAT, NS), obs_ens, y_obs.reshape(16, 128),
+                obs_rinv.reshape(16, 128), block_list.T, loc_class.T, patch_active[None, :],
+                loc_table[None, :],
+            )
+        ],
     )
     return out.reshape(MEM, PAT, NS)
 

time: 82 us -> 79.7 us (0.972)
  the two profiles are of different devices: /device:TPU:3 before, /device:TPU:1 now
where the time goes in v4:
time: 79.7 us; the launch traced here: 79.5 us
  Pallas kernels  78.8 us (99%)
    pallas_call x1, Pallas kernels, per_device(): pl.pallas_call(kernel, out_shape=jax.ShapeDtypeStruct((MEM * PAT, NS), BF...  78.8 us

profile of v4, /device:TPU:1, one launch (start us, length us, event | category | flops | bytes accessed | tf_op | source)
XLA Modules:
  0.0 79.5 jit_solution(1132595201250394031)
XLA Ops:
  0.0 78.8 %shard_map.82 = bf16[512,256]{1,0:T(8,128)(2,1)S(1)} custom-call(bf16[512,256]{1,0:T(8,128)(2,1)} %bitcast.9, bf16[8,2048]{1,0:T(8,128)(2,1)} %obs_hbm.1, bf16[16,128]{1,0:T(8,128)(2,1)} %bitcast.10, bf16[16,128]{1,0:T(8,128)(2,1)} %bitcast.11, s32[8,64]{1,0:T(8,128)} %bitcast.12, s32[8,64]{1,0:T(8,128)} %bitcast.13, s32[1,64]{1,0:T(1,128)} %bitcast.14, ...), custom_call_target="tpu_custom_call" | custom-call | flops 4000000000 | bytes 2000000 | tf_op jit(solution)/shard_map/pallas_call | solution.py:338
  78.8 0.7 copy.10

commit v5 on v4

--- a/solution.py
+++ b/solution.py
@@ -69,7 +69,7 @@
     return value.reshape(N, MEM, value.shape[-1]).astype(BF16)
 
 
-def analyse(obs, values, table, y_it, z_it):
+def analyse(obs, values, table, y_it, z_it, beside):
     def column_of(at, step):
         return jnp.concatenate([values[:, at + step * k:at + step * k + 1] for k in range(CUT)], 0)
 
@@ -101,12 +101,14 @@
         return carry
 
     lax.fori_loop(0, NEWTON - 2, step, 0)
+    other = beside()
     y, z = split(y_it[...]), split(z_it[...])
     last = dot3(split(1.5 * eye - 0.5 * dot3(z, y)), z)
     z = split(last)
-    inner = dot3(z, split(jnp.broadcast_to(projected, (COUNT, COUNT))), NT)
+    inner = dot3(z, split(jnp.broadcast_to(projected, (128, COUNT))), NT)
     shift = dot3(z, split(inner)) / (fro * (COUNT - 1))
-    return (last / jnp.sqrt(fro) + shift).astype(BF16)
+    shift = jnp.concatenate([shift, shift], axis=1)
+    return (last / jnp.sqrt(fro) + shift).astype(BF16), other
 
 
 def level(group):
@@ -126,7 +128,7 @@
 def kernel(
     state_hbm, obs_hbm, y_hbm, rinv_hbm, list_hbm, class_hbm, active_hbm, table_hbm, out_ref,
     state, obs_in, y_in, rinv_in, list_in, class_in, active_in, table_in,
-    send1, relay, send_s, relay_s, send2, recv2, recv_s, send3, recv3, send_r, recv_r, choose, y_it, z_it,
+    send1, relay, send_s, relay_s, send2, recv2, recv_s, send3, recv3, send_r, recv_r, choose, back_to, y_it, z_it,
     in_sem, s1_sem, r1_sem, sp_sem, rp_sem, s2_sem, r2_sem, ss_sem, rs_sem, s3_sem, r3_sem, sr_sem, rr_sem,
 ):
     group, me = lax.axis_index("domain"), lax.axis_index("member")
@@ -206,11 +208,15 @@
     tile_of = one_hot(iota(narrow, 1) == 2 * (me % 8) + (iota(narrow, 0) % MEM) // 4)
     for values in (y_in, rinv_in):
         tile = dot(tile_of, values[...])
-        parts.append(jnp.where(ours & (spot == member % 4), tile, 0.0).astype(BF16))
+        for cut in range(CUT):
+            wanted = member % 4 // CUT * CUT + cut
+            parts.append(jnp.where(ours & (spot == wanted), tile, 0.0).astype(BF16))
     tall = (WIDTH, SLAB)
     at = iota(tall, 0)
     goal = (at // 128) * (2 * CUT) + ((at % 128) // BROWS) * CUT + at % CUT
-    place = [one_hot(iota(tall, 1) == goal)] + [one_hot(lane[:128] == a) for a in (Y_AT, R_AT)]
+    place = [one_hot(iota(tall, 1) == goal)] + [
+        one_hot(lane[:128] == a) for a in (Y_AT, Y_AT + SIDE, R_AT, R_AT + SIDE)
+    ]
     packed = dot(jnp.concatenate(parts, axis=1), jnp.concatenate(place, axis=0))
     packed = jnp.where(lane == ID_AT, jnp.concatenate([ids] * N, axis=0), packed)
     packed = jnp.where(lane == KIND_AT, jnp.concatenate([kinds] * N, axis=0), packed)
@@ -228,7 +234,7 @@
     square = (SLAB, SLAB)
     source, goal = iota(square, 0), iota(square, 1)
     plain = source == goal
-    value = plain & ((goal == Y_AT) | (goal == R_AT))
+    value = plain & ((goal == Y_AT) | (goal == R_AT) | (goal >= Y_AT + SIDE))
     turn = me // 8
     mix = jnp.concatenate(
         [
@@ -271,16 +277,12 @@
     value_at = jnp.where(
         low, OWN + inner + OWN, jnp.where(high, inner - OWN + 2 * OWN, inner)
     )
-    values = []
     for cut in range(CUT):
         hot = one_hot(iota((COUNT, SLAB), 1) == column_at + cut)
         picked = slabs(dot_dims(hot, held, NT))
         send3[:, 2 * cut] = picked[:, :, 0:128]
         send3[:, 2 * cut + 1] = picked[:, :, 128:256]
-        hot = one_hot(iota((COUNT, COUNT), 1) == value_at + cut)
-        values.append(dot(hot, held))
-    turned = dot(values[1].astype(BF16), one_hot(source == goal - SIDE))
-    values = jnp.where(lane < Y_AT + SIDE, values[0], turned)
+    values = dot(one_hot(iota((COUNT, COUNT), 1) == value_at), held)
     send3[:, 2 * CUT] = slabs(jnp.where(lane == KIND_AT, kinds, values))
     plane(send3, recv3, s3_sem, r3_sem)
 
@@ -295,11 +297,14 @@
         ],
         axis=1,
     )
-    transform = analyse(obs, part(2 * CUT), table_in[...], y_it, z_it)
-    arrived(recv_s, rs_sem)
-    members = flat(recv_s)
-    mean = jnp.sum(members, axis=0, keepdims=True) / COUNT
-    update = dot_dims(transform, (members - mean).astype(BF16), TN)
+    def centred():
+        arrived(recv_s, rs_sem)
+        members = flat(recv_s)
+        mean = jnp.sum(members, axis=0, keepdims=True) / COUNT
+        return mean, (members - mean).astype(BF16)
+
+    transform, (mean, pert) = analyse(obs, part(2 * CUT), table_in[...], y_it, z_it, centred)
+    update = dot_dims(transform, pert, TN)
     send_r[...] = slabs(mean + update)
     for k in FAR_FIRST:
         to = lax.rem(me + k, N)
@@ -316,14 +321,17 @@
 
     ones = jnp.ones((COUNT, NS), BF16)
     analysed = dot_dims(choose[...], ones, TN) > 0.5
+    eye = one_hot(iota((COUNT, COUNT), 0) == iota((COUNT, COUNT), 1))
+    back_to[...] = dot_dims(choose[...], eye, TN).astype(BF16)
+    out_ref[...] = jnp.where(analysed, 0.0, state[...].astype(F32)).astype(BF16)
     sent(send1, s1_sem)
     sent(send_s, sp_sem)
     sent(send2, s2_sem)
     sent(relay_s, ss_sem)
     sent(send3, s3_sem)
     arrived(recv_r, rr_sem)
-    back = dot_dims(choose[...], flat(recv_r).astype(BF16), TN)
-    out_ref[...] = jnp.where(analysed, back, state[...].astype(F32)).astype(BF16)
+    back = dot(back_to[...], flat(recv_r).astype(BF16))
+    out_ref[...] = (out_ref[...].astype(F32) + back).astype(BF16)
     sent(send_r, sr_sem)
 
     @pl.when(jnp.logical_not(home))
@@ -361,6 +369,7 @@
             slab,
             slab,
             pltpu.VMEM((COUNT, MEM * PAT), BF16),
+            pltpu.VMEM((MEM * PAT, COUNT), BF16),
             pltpu.VMEM((COUNT, COUNT), F32),
             pltpu.VMEM((COUNT, COUNT), F32),
             pltpu.SemaphoreType.DMA((8,)),

time: 79.7 us -> 79.5 us (level)
  no operation moved by 1% of the time
where the time goes in v5:
time: 79.5 us; the launch traced here: 79.4 us
  Pallas kernels  78.7 us (99%)
    pallas_call x1, Pallas kernels, per_device(): pl.pallas_call(kernel, out_shape=jax.ShapeDtypeStruct((MEM * PAT, NS), BF...  78.7 us

profile of v5, /device:TPU:1, one launch (start us, length us, event | category | flops | bytes accessed | tf_op | source)
XLA Modules:
  0.0 79.4 jit_solution(4921590351596252001)
XLA Ops:
  0.0 78.7 %shard_map.82 = bf16[512,256]{1,0:T(8,128)(2,1)S(1)} custom-call(bf16[512,256]{1,0:T(8,128)(2,1)} %bitcast.9, bf16[8,2048]{1,0:T(8,128)(2,1)} %obs_hbm.1, bf16[16,128]{1,0:T(8,128)(2,1)} %bitcast.10, bf16[16,128]{1,0:T(8,128)(2,1)} %bitcast.11, s32[8,64]{1,0:T(8,128)} %bitcast.12, s32[8,64]{1,0:T(8,128)} %bitcast.13, s32[1,64]{1,0:T(1,128)} %bitcast.14, ...), custom_call_target="tpu_custom_call" | custom-call | flops 4000000000 | bytes 2000000 | tf_op jit(solution)/shard_map/pallas_call | solution.py:346
  78.7 0.7 copy.10
